TPU v7x, 32 devices: a whole 2x2x4 slice. The times are simulated.
32 devices in a mesh: fsdp: 16 (over z, y, core), ctx: 2 (over x).
Axes of the slice: x: 2, y: 2, z: 4, core: 2. Of those that a mesh axis runs over, the one named last changes fastest.
Arguments:
- hidden: bfloat16 [16, 512, 5120], P('fsdp', 'ctx'), may hold values from -6 to 6
- queries: bfloat16 [16, 512, 4096], P('fsdp', 'ctx'), may hold values from -300 to 300, as said below
- norm_gain: float32 [5120], replicated, may hold values from 0.1 to 1.9
- key_gain: float32 [128], replicated, may hold values from 0.1 to 1.9
- k_weight: bfloat16 [5120, 512], P('fsdp'), may hold values from -0.078125 to 0.078125
- v_weight: bfloat16 [5120, 512], P('fsdp'), may hold values from -0.078125 to 0.078125
- segment: int32 [16, 512], P('fsdp', 'ctx'), may hold values from 0 to 3, as said below
- position: int32 [16, 512], P('fsdp', 'ctx'), may hold values from 0 to 8191, as said below
Outputs:
- attended: bfloat16 [16, 512, 4096], P('fsdp', 'ctx')
Inputs may be any that keep to these rules, and one draw needn't show every extreme that they name: queries keep to the stated range. `segment`: in each stretch, read in the tokens' order, rollout numbers never fall; the tokens of a stretch lie in its slots in an order that keeps 256 slots on each index of ctx, one token of every 2 consecutive ones on each. `position`: within one rollout of a stretch positions rise by one from token to token.
All inputs are finite; a program needn't handle non-finite values.
Results may differ from a plain program's by a relative error of at most 0.0075.
The roundings to bfloat16 on the way count: a program that leaves them out, or rounds other values in their place, can miss the bound.
Values may be sent and summed in bfloat16 or wider, within the bound.
No kernel may reach another device: no remote copies, remote signals or barrier semaphores. Data moves between devices by JAX's collectives and lax.ppermute only.
A program may use at most 192 MiB of HBM per device.

v0:
```python
import math

import jax
import jax.numpy as jnp
from jax import lax
from jax.sharding import PartitionSpec as P

KVH = 4
HD = 128
G = 8


EPS = 1e-06
THETA = 1000000.0


def rotate(values_in, where):
    width = values_in.shape[-1]
    half = width // 2
    freq = jnp.exp(jnp.arange(half, dtype=jnp.float32) * (-2.0 * math.log(THETA) / width))
    angle = where.astype(jnp.float32)[:, None] * freq[None, :]
    cosine = jnp.cos(angle)[:, None, :]
    sine = jnp.sin(angle)[:, None, :]
    first = values_in[..., :half]
    second = values_in[..., half:]
    return jnp.concatenate(
        [first * cosine - second * sine, second * cosine + first * sine], axis=-1
    )


def on_device(hidden, queries, norm_gain, key_gain, k_weight, v_weight, segment, position):
    rows_here = hidden.shape[1]
    inputs = hidden[0].astype(jnp.float32)
    normed = (
        inputs * lax.rsqrt(jnp.mean(inputs * inputs, axis=-1, keepdims=True) + EPS) * norm_gain
    ).astype(jnp.bfloat16)
    key_sums = jnp.dot(
        normed,
        lax.all_gather(k_weight, "fsdp", axis=0, tiled=True),
        preferred_element_type=jnp.float32,
    )
    value_sums = jnp.dot(
        normed,
        lax.all_gather(v_weight, "fsdp", axis=0, tiled=True),
        preferred_element_type=jnp.float32,
    )
    raw = key_sums.reshape(rows_here, KVH, HD)
    normk = raw * lax.rsqrt(jnp.mean(raw * raw, axis=-1, keepdims=True) + EPS) * key_gain
    keys = rotate(normk, position[0]).astype(jnp.bfloat16)
    values = value_sums.reshape(rows_here, KVH, HD).astype(jnp.bfloat16)
    grouped = queries[0].reshape(rows_here, KVH, G, HD)
    own_seg = segment[0]
    own_pos = position[0]
    scale = 1.0 / math.sqrt(HD)
    running = jnp.full((KVH, G, rows_here), -1e30, jnp.float32)
    key_piece = lax.all_gather(keys[None], "ctx", axis=1, tiled=True)
    value_piece = lax.all_gather(values[None], "ctx", axis=1, tiled=True)
    seg_piece = lax.all_gather(segment, "ctx", axis=1, tiled=True)
    pos_piece = lax.all_gather(position, "ctx", axis=1, tiled=True)
    scores = (
        jnp.einsum("tkgd,skd->kgts", grouped, key_piece[0], preferred_element_type=jnp.float32)
        * scale
    )
    allowed = (seg_piece[0][None, :] == own_seg[:, None]) & (
        pos_piece[0][None, :] <= own_pos[:, None]
    )
    scores = jnp.where(allowed, scores, -1e30)
    newest = jnp.maximum(running, jnp.max(scores, axis=-1))
    weights = jnp.where(allowed, jnp.exp(scores - newest[..., None]), 0.0)
    rounded = weights.astype(jnp.bfloat16)
    total = jnp.sum(weights, axis=-1)
    summed = jnp.einsum(
        "kgts,skd->kgtd", rounded, value_piece[0], preferred_element_type=jnp.float32
    )
    running, total, summed = (newest, total, summed)
    result = summed / total[..., None]
    result = (
        jnp.transpose(result, (2, 0, 1, 3)).reshape(rows_here, KVH * G * HD).astype(jnp.bfloat16)
    )
    return result[None]


def solution(mesh):
    placed = (
        P("fsdp", "ctx", None),
        P("fsdp", "ctx", None),
        P(),
        P(),
        P("fsdp", None),
        P("fsdp", None),
        P("fsdp", "ctx"),
        P("fsdp", "ctx"),
    )
    return jax.shard_map(
        on_device, mesh=mesh, in_specs=placed, out_specs=P("fsdp", "ctx", None), check_vma=False
    )
```

profile of v0, /device:TPU:0, one launch (start us, length us, event | category | flops | bytes accessed | tf_op | source)
XLA Modules:
  0.0 162.6 jit_solution(3349275097497338881)
XLA Ops:
  6.5 0.0 copy-start.1
  6.5 0.0 copy-start.2
  6.5 0.0 all-gather.4.cloned.1.call-start
  6.5 0.7 all-gather.4.cloned.1.call-update
  7.3 0.0 all-gather.6.cloned.1.call-start
  7.3 0.7 all-gather.6.cloned.1.call-update
  8.0 0.0 copy-start
  8.0 0.8 convert_element_type.50
  8.9 2.1 %copy.21 = bf16[32,8,32,128]{3,2,1,0:T(8,128)(2,1)S(1)} copy(bf16[32,8,32,128]{3,1,2,0:T(8,128)(2,1)} %bitcast.68) | data formatting | bytes 4194304
  10.9 5.4 %all_gather.19 = s32[1,512]{1,0:T(1,128)S(1)} all-gather(s32[1,256]{1,0:T(1,128)} %param.15), channel_id=1, replica_groups=mesh['fsdp'=16,'ctx'=2] {'ctx'}, dimensions={1}, use_global_device_ids=true | all-gather | bytes 3072 | tf_op jit(solution)/shard_map/all_gather | solution.py:59
  16.3 4.4 %all_gather.18 = s32[1,512]{1,0:T(1,128)S(1)} all-gather(s32[1,256]{1,0:T(1,128)} %param.14), channel_id=1, replica_groups=mesh['fsdp'=16,'ctx'=2] {'ctx'}, dimensions={1}, use_global_device_ids=true | all-gather | bytes 3072 | tf_op jit(solution)/shard_map/all_gather | solution.py:58
  20.8 0.0 copy-done
  20.8 0.6 fusion.6
  21.4 0.3 multiply_cosine_fusion
  21.7 0.0 copy-done.1
  21.7 0.0 copy-done.2
  21.8 0.2 compare_and_fusion
  22.0 46.4 %all-gather.4.cloned.1.call-done = bf16[5120,512]{1,0:T(8,128)(2,1)} async-done(((bf16[320,512]{1,0:T(8,128)(2,1)}), bf16[5120,512]{1,0:T(8,128)(2,1)}) %all-gather.4.cloned.1.call-update) | async-done | bytes 5242896 | tf_op jit(solution)/shard_map/all_gather | solution.py:39
  68.4 0.0 copy-start.4
  68.4 7.9 %copy.9 = bf16[512,5120]{1,0:T(8,128)(2,1)} copy(bf16[512,5120]{0,1:T(8,128)(2,1)} %bitcast.66) | data formatting | bytes 10485760 | tf_op jit(solution)/shard_map/dot_general | solution.py:37
  76.3 0.0 copy-done.4
  76.3 0.0 copy-start.3
  76.3 5.2 %multiply_reduce_fusion = (f32[256,4]{0,1:T(4,128)S(1)}, f32[256,4,128]{0,2,1:T(8,128)S(1)}) fusion(bf16[4,128,5120]{2,1,0:T(8,128)(2,1)} %bitcast.67, bf16[1,256,5120]{2,1,0:T(8,128)(2,1)} %param.8, f32[5120]{0:T(1024)S(1)} %copy-done.4, f32[256]{0:T(256)S(1)} %add_rsqrt_fusion.1), kind=kOutput, calls=%fused_computation.25 | convolution fusion | flops 1347681280 | bytes 8414208 | tf_op jit(solution)/shard_map/dot_general | solution.py:37
  81.4 0.0 copy-done.3
  81.5 0.1 multiply_multiply_fusion
  81.6 0.1 fusion.26
  81.7 9.2 %all_gather.21 = bf16[1,512,4,128]{1,3,2,0:T(8,128)(2,1)S(1)} all-gather(bf16[1,256,4,128]{1,3,2,0:T(8,128)(2,1)S(1)} %pad_maximum_fusion), channel_id=1, replica_groups=mesh['fsdp'=16,'ctx'=2] {'ctx'}, dimensions={1}, use_global_device_ids=true | all-gather | bytes 786432 | tf_op jit(solution)/shard_map/all_gather | solution.py:56
  90.8 34.4 %all-gather.6.cloned.1.call-done = bf16[5120,512]{1,0:T(8,128)(2,1)} async-done(((bf16[320,512]{1,0:T(8,128)(2,1)}), bf16[5120,512]{1,0:T(8,128)(2,1)}) %all-gather.6.cloned.1.call-update) | async-done | bytes 5242896 | tf_op jit(solution)/shard_map/all_gather | solution.py:44
  125.2 5.6 %fusion.18 = bf16[256,4,128]{0,2,1:T(8,128)(2,1)S(1)} fusion(bf16[1,256,5120]{2,1,0:T(8,128)(2,1)} %param.8, f32[5120]{0:T(1024)S(1)} %copy-done.4, f32[256]{0:T(256)S(1)} %add_rsqrt_fusion.1, bf16[5120,512]{1,0:T(8,128)(2,1)} %all-gather.6.cloned.1.call-done), kind=kOutput, calls=%fused_computation.20 | convolution fusion | flops 1347551232 | bytes 8147968 | tf_op jit(solution)/shard_map/dot_general | solution.py:42
  130.9 9.3 %all-gather = bf16[512,4,128]{0,2,1:T(8,128)(2,1)S(1)} all-gather(bf16[256,4,128]{0,2,1:T(8,128)(2,1)S(1)} %fusion.18), channel_id=2, replica_groups=mesh['fsdp'=16,'ctx'=2] {'ctx'}, dimensions={0}, use_global_device_ids=true | all-gather | bytes 786432 | tf_op jit(solution)/shard_map/all_gather | solution.py:57
  140.2 3.8 %fusion = (f32[4,8,256]{2,1,0:T(8,128)S(1)}, f32[4,512,256,8]{2,1,3,0:T(8,128)S(1)}) fusion(pred[256,512]{0,1:T(8,128)(4,1)S(1)} %compare_and_fusion, bf16[256,4,8,128]{3,2,1,0:T(8,128)(2,1)S(1)} %bitcast.65, bf16[1,512,4,128]{1,3,2,0:T(8,128)(2,1)S(1)} %all_gather.21), kind=kOutput, calls=%fused_computation.2 | convolution fusion | flops 1086316544 | bytes 19562496 | tf_op jit(solution)/shard_map/tkgd,skd->kgts/dot_general | solution.py:61
  144.1 4.2 %fusion.1 = f32[4,8,256]{2,1,0:T(8,128)S(1)} fusion(f32[4,512,256,8]{2,1,3,0:T(8,128)S(1)} %get-tuple-element.12, f32[4,8,256]{2,1,0:T(8,128)S(1)} %broadcast_maximum_fusion, pred[256,512]{0,1:T(8,128)(4,1)S(1)} %compare_and_fusion), kind=kLoop, calls=%fused_computation.3 | loop fusion | flops 20963328 | bytes 16973824 | tf_op jit(solution)/shard_map/reduce_sum | solution.py:71
  148.3 4.6 %fusion.12 = bf16[256,4,8,128]{0,3,2,1:T(8,128)(2,1)S(1)} fusion(f32[4,512,256,8]{2,1,3,0:T(8,128)S(1)} %get-tuple-element.12, f32[4,8,256]{2,1,0:T(8,128)S(1)} %broadcast_maximum_fusion, pred[256,512]{0,1:T(8,128)(4,1)S(1)} %compare_and_fusion, f32[256,4,8]{0,2,1:T(8,128)S(1)} %bitcast.70, bf16[512,4,128]{0,2,1:T(8,128)(2,1)S(1)} %all-gather), kind=kOutput, calls=%fused_computation.16 | convolution fusion | flops 1096810496 | bytes 19595264 | tf_op jit(solution)/shard_map/kgts,skd->kgtd/dot_general | solution.py:72
  152.9 2.9 %copy.13 = bf16[1,256,4096]{2,1,0:T(8,128)(2,1)} copy(bf16[1,256,4096]{1,2,0:T(8,128)(2,1)S(1)} %bitcast.69) | data formatting | bytes 4194304 | tf_op jit(solution)/shard_map/convert_element_type | solution.py:78
  (5 shorter events, 0.0 us)
Async XLA Ops:
  6.5 15.2 %copy-start.1 = (s32[1,256]{1,0:T(1,128)S(1)}, s32[1,256]{1,0:T(1,128)}, u32[]{:S(2)}) copy-start(s32[1,256]{1,0:T(1,128)} %param.15) | copy-start | bytes 3076
  6.5 15.2 %copy-start.2 = (s32[1,256]{1,0:T(1,128)S(1)}, s32[1,256]{1,0:T(1,128)}, u32[]{:S(2)}) copy-start(s32[1,256]{1,0:T(1,128)} %param.14) | copy-start | bytes 3076
  6.5 61.8 %all-gather.4.cloned.1.call-start = ((), (), s32[]{:S(2)}) async-start(), calls=%async_computation | async-start | bytes 5570560 | tf_op jit(solution)/shard_map/all_gather | solution.py:39
  7.3 118.0 %all-gather.6.cloned.1.call-start = ((), (), s32[]{:S(2)}) async-start(), calls=%async_computation.1 | async-start | bytes 5570560 | tf_op jit(solution)/shard_map/all_gather | solution.py:44
  8.0 12.8 %copy-start = (bf16[1,256,5120]{2,1,0:T(8,128)(2,1)S(1)}, bf16[1,256,5120]{2,1,0:T(8,128)(2,1)}, u32[]{:S(2)}) copy-start(bf16[1,256,5120]{2,1,0:T(8,128)(2,1)} %param.8) | copy-start | bytes 7864324
  68.4 7.9 %copy-start.4 = (f32[5120]{0:T(1024)S(1)}, f32[5120]{0:T(1024)}, u32[]{:S(2)}) copy-start(f32[5120]{0:T(1024)} %param.10) | copy-start | bytes 61444
  76.3 5.2 %copy-start.3 = (f32[128]{0:T(128)S(1)}, f32[128]{0:T(128)}, u32[]{:S(2)}) copy-start(f32[128]{0:T(128)} %param.11) | copy-start | bytes 1540
Sparse Core Ops, SparseCore 0:
  9.6 58.6 all-gather.3
  70.6 54.5 all-gather.5
where the time goes:
time: 163 us
  waiting for transfers between devices  82.2 us (50%)
  blocking collectives  28.3 us (17%)
  matrix products  19.2 us (12%)
  between operations  13.5 us (8%)
  local copies, waits for them, and re-layouts  12.8 us (8%)
  other arithmetic  6.39 us (4%)
    all_gather x1, waiting for transfers between devices, on_device(): lax.all_gather(k_weight, 'fsdp', axis=0, tiled=True)  46.4 us
    all_gather x1, waiting for transfers between devices, on_device(): lax.all_gather(v_weight, 'fsdp', axis=0, tiled=True)  34.4 us
    all_gather x1, blocking collectives, on_device(): value_piece = lax.all_gather(values[None], 'ctx', axis=1, tiled=True)  9.33 us
    all_gather x1, blocking collectives, on_device(): key_piece = lax.all_gather(keys[None], 'ctx', axis=1, tiled=True)  9.16 us
    dot_general x1, local copies, waits for them, and re-layouts, on_device(): jnp.dot(normed, lax.all_gather(k_weight, 'fsdp', axis=0, tiled=True), pre...  7.9 us
    dot_general x1, matrix products, on_device(): jnp.dot(normed, lax.all_gather(v_weight, 'fsdp', axis=0, tiled=True), pre...  5.62 us
    all_gather x1, blocking collectives, on_device(): pos_piece = lax.all_gather(position, 'ctx', axis=1, tiled=True)  5.42 us
    dot_general x1, matrix products, on_device(): jnp.dot(normed, lax.all_gather(k_weight, 'fsdp', axis=0, tiled=True), pre...  5.15 us
  transfers between devices with their start and end apart: 2, of which 2 were waited for; matrix products, arithmetic and copies ran while one was open for 11% of the time, Pallas kernels for 0%

commit v1 on v0

v1 whole, which is shorter than its diff:
```python
import functools
import math

import jax
import jax.numpy as jnp
from jax import lax
from jax.experimental import pallas as pl
from jax.experimental.pallas import tpu as pltpu
from jax.sharding import PartitionSpec as P

KVH = 4
HD = 128
G = 8
EPS = 1e-06
THETA = 1000000.0
MASKED = -1e30
VMEM_LIMIT = 48 * 2**20
AXES = ("fsdp", "ctx")


def project_kernel(chips_z, count, place, own, other, cosine, sine, gain, *rest):
    pieces, (kv_own, kv_other, weight, acc, sems) = rest[: 5 * chips_z], rest[5 * chips_z :]
    z, y, x = place[0], place[1], place[2]
    rows = weight.shape[2]
    copies = []
    for k in range(chips_z):
        p = lax.rem(z - k + chips_z, chips_z)
        near, far = p * 2 + y, p * 2 + 1 - y
        mine, across, beside, top, bottom = pieces[5 * k : 5 * k + 5]
        targets = (
            (mine, weight.at[near, x]),
            (across, weight.at[near, 1 - x]),
            (beside, weight.at[far, x]),
            (top, weight.at[far, 1 - x, pl.ds(0, rows // 2)]),
            (bottom, weight.at[far, 1 - x, pl.ds(rows // 2, rows // 2)]),
        )
        started = []
        for i, (source, target) in enumerate(targets):
            copy = pltpu.make_async_copy(source, target, sems.at[k, i])
            copy.start()
            started.append(copy)
        copies.append((near, started[:2]))
        copies.append((far, started[2:]))
    for step, (chunk, waits) in enumerate(copies):
        for copy in waits:
            copy.wait()
        for half in range(2):
            for part, lhs in enumerate((own, other)):
                term = jnp.dot(
                    lhs[chunk], weight[chunk, half], preferred_element_type=jnp.float32
                )
                at = pl.ds(part * count, count)
                if step == 0:
                    acc[half, at, :] = term
                else:
                    acc[half, at, :] += term
    for half in range(2):
        for part, out in enumerate((kv_own, kv_other)):
            at = pl.ds(part * count, count)
            raw = acc[half, at, :HD]
            normk = raw * lax.rsqrt(jnp.mean(raw * raw, axis=-1, keepdims=True) + EPS) * gain[...]
            turned = normk * cosine[at, :] + pltpu.roll(normk, HD // 2, 1) * sine[at, :]
            out[:, half * 2 * HD : half * 2 * HD + HD] = turned.astype(jnp.bfloat16)
            out[:, half * 2 * HD + HD : (half + 1) * 2 * HD] = acc[half, at, HD:].astype(
                jnp.bfloat16
            )


def attend_kernel(pieces, count, place, queries, seg_q, pos_q, seg_k, pos_k, *rest):
    sources, (out, bias, keys, values) = rest[: 2 * pieces], rest[2 * pieces :]
    step = pl.program_id(0)

    @pl.when(step == 0)
    def _():
        allowed = (seg_k[...] == seg_q[...]) & (pos_k[...] <= pos_q[...])
        bias[...] = jnp.where(allowed, 0.0, MASKED)

    for at in range(KVH):

        @pl.when(step == at)
        def _():
            left = (at % 2) * 2 * HD
            for i in range(pieces):
                source = sources[(at // 2) * pieces + i]
                keys[i * count : (i + 1) * count, :] = source[:, left : left + HD]
                values[i * count : (i + 1) * count, :] = source[:, left + HD : left + 2 * HD]

    factor = math.log2(math.e) / math.sqrt(HD)
    for g in range(G):
        part = slice(g * HD, (g + 1) * HD)
        scores = lax.dot_general(
            queries[:, part], keys[...], (((1,), (1,)), ((), ())),
            preferred_element_type=jnp.float32,
        ) + bias[...]
        top = jnp.max(scores, axis=-1, keepdims=True)
        weights = jnp.exp2((scores - top) * factor)
        total = jnp.sum(weights, axis=-1, keepdims=True)
        summed = jnp.dot(
            weights.astype(jnp.bfloat16), values[...], preferred_element_type=jnp.float32
        )
        out[:, part] = (summed * (1.0 / total)).astype(jnp.bfloat16)


def on_device(
    n, m, hidden, queries, norm_gain, key_gain, k_weight, v_weight, segment, position
):
    count, width = hidden.shape[1:]
    rows = 2 * k_weight.shape[0]
    chips_z = n // 4
    chunks = n // 2
    mine_f, mine_c = lax.axis_index("fsdp"), lax.axis_index("ctx")
    z, y, core, x = mine_f // 4, (mine_f // 2) % 2, mine_f % 2, mine_c % 2

    def send(array, move):
        pairs = []
        for f in range(n):
            for c in range(m):
                g, d = move(f, c)
                pairs.append((f * m + c, (g % n) * m + d % m))
        return lax.ppermute(array, AXES, pairs)

    def to_core(array):
        return send(array, lambda f, c: (f ^ 1, c))

    def to_y(array):
        return send(array, lambda f, c: (f ^ 2, c))

    def to_x(array):
        return send(array, lambda f, c: (f, c ^ 1))

    def to_z(array, k):
        return send(array, lambda f, c: (f + 4 * k, c))

    both = jnp.concatenate(
        [k_weight.reshape(-1, KVH, HD), v_weight.reshape(-1, KVH, HD)], axis=2
    ).reshape(-1, 2, 4 * HD)
    kept = jnp.where(core == 0, both[:, 0], both[:, 1])
    given = jnp.where(core == 0, both[:, 1], both[:, 0])
    taken = to_core(given)
    chip = jnp.where(
        core == 0, jnp.concatenate([kept, taken]), jnp.concatenate([taken, kept])
    )
    first, second = chip[:, : 2 * HD], chip[:, 2 * HD :]
    half_x = jnp.where(x == 0, first, second)
    half_o = jnp.where(x == 0, second, first)

    inputs = hidden[0].astype(jnp.float32)
    normed = (
        inputs * lax.rsqrt(jnp.mean(inputs * inputs, axis=-1, keepdims=True) + EPS) * norm_gain
    ).astype(jnp.bfloat16)
    normed = normed.reshape(count, chunks, rows).transpose(1, 0, 2)
    normed_other = to_core(normed)

    ints = jnp.concatenate([segment, position])
    ints_all = [ints] + [send(ints, lambda f, c, d=d: (f, c + d)) for d in range(1, m)]
    position_other = to_core(position)
    where = jnp.concatenate([position[0], position_other[0]]).astype(jnp.float32)
    half = HD // 2
    freq = jnp.exp(jnp.arange(half, dtype=jnp.float32) * (-2.0 * math.log(THETA) / HD))
    angle = where[:, None] * freq[None, :]
    cosine, sine = jnp.cos(angle), jnp.sin(angle)
    cosine = jnp.concatenate([cosine, cosine], axis=1)
    sine = jnp.concatenate([-sine, sine], axis=1)

    pieces = []
    mine = [half_x] + [to_z(half_x, k) for k in range(1, chips_z)]
    for k in range(chips_z):
        beside = to_y(mine[k])
        if k == 0:
            across = half_o
            top, bottom = to_x(beside[: rows // 2]), to_x(beside[rows // 2 :])
        else:
            across = to_x(mine[k])
            top, bottom = to_x(beside[: rows // 2]), to_y(across[rows // 2 :])
        pieces += [mine[k], across, beside, top, bottom]

    place = jnp.stack([z, y, x]).astype(jnp.int32)
    smem = pl.BlockSpec(memory_space=pltpu.SMEM)
    vmem = pl.BlockSpec(memory_space=pltpu.VMEM)
    anywhere = pl.BlockSpec(memory_space=pl.ANY)
    kv_own, kv_other = pl.pallas_call(
        functools.partial(project_kernel, chips_z, count),
        out_shape=[jax.ShapeDtypeStruct((count, 4 * HD), jnp.bfloat16)] * 2,
        in_specs=[smem] + [vmem] * 5 + [anywhere] * len(pieces),
        out_specs=[vmem] * 2,
        scratch_shapes=[
            pltpu.VMEM((chunks, 2, rows, 2 * HD), jnp.bfloat16),
            pltpu.VMEM((2, 2 * count, 2 * HD), jnp.float32),
            pltpu.SemaphoreType.DMA((chips_z, 5)),
        ],
        compiler_params=pltpu.CompilerParams(vmem_limit_bytes=VMEM_LIMIT),
        cost_estimate=pl.CostEstimate(
            flops=2 * 2 * count * width * 4 * HD,
            bytes_accessed=2 * width * (2 * count + 4 * HD),
            transcendentals=0,
        ),
        name="project",
    )(place, normed, normed_other, cosine, sine, key_gain[None], *pieces)

    sources = [kv_own] + [send(kv_own, lambda f, c, d=d: (f, c + d)) for d in range(1, m)]
    sources += [send(kv_other, lambda f, c, d=d: (f ^ 1, c + d)) for d in range(m)]
    seg_k = jnp.concatenate([piece[:1] for piece in ints_all], axis=1)
    pos_k = jnp.concatenate([piece[1:] for piece in ints_all], axis=1)

    def block(step, place):
        return (0, lax.rem(step + 2 * place[0], KVH))

    whole = pl.BlockSpec(memory_space=pltpu.VMEM)
    result = pl.pallas_call(
        functools.partial(attend_kernel, m, count),
        out_shape=jax.ShapeDtypeStruct((count, KVH * G * HD), jnp.bfloat16),
        grid_spec=pltpu.PrefetchScalarGridSpec(
            num_scalar_prefetch=1,
            grid=(KVH,),
            in_specs=[pl.BlockSpec((count, G * HD), block)] + [whole] * (4 + 2 * m),
            out_specs=pl.BlockSpec((count, G * HD), block),
            scratch_shapes=[
                pltpu.VMEM((count, m * count), jnp.float32),
                pltpu.VMEM((m * count, HD), jnp.bfloat16),
                pltpu.VMEM((m * count, HD), jnp.bfloat16),
            ],
        ),
        compiler_params=pltpu.CompilerParams(vmem_limit_bytes=VMEM_LIMIT),
        cost_estimate=pl.CostEstimate(
            flops=4 * count * m * count * KVH * G * HD,
            bytes_accessed=4 * count * KVH * G * HD,
            transcendentals=count * m * count * KVH * G,
        ),
        name="attend",
    )(
        core.astype(jnp.int32)[None],
        queries[0],
        segment.reshape(count, 1),
        position.reshape(count, 1),
        seg_k,
        pos_k,
        *sources,
    )
    return result[None]


def solution(mesh):
    placed = (
        P("fsdp", "ctx", None),
        P("fsdp", "ctx", None),
        P(),
        P(),
        P("fsdp", None),
        P("fsdp", None),
        P("fsdp", "ctx"),
        P("fsdp", "ctx"),
    )
    return jax.shard_map(
        functools.partial(on_device, mesh.shape["fsdp"], mesh.shape["ctx"]),
        mesh=mesh,
        in_specs=placed,
        out_specs=P("fsdp", "ctx", None),
        check_vma=False,
    )
```

time: 163 us -> 119 us (0.73)
  the two profiles are of different devices: /device:TPU:0 before, /device:TPU:24 now
where the time goes in v1:
time: 119 us
  waiting for transfers between devices  52.2 us (44%)
  starting transfers between devices  25.4 us (21%)
  Pallas kernels  20.9 us (18%)
  local copies, waits for them, and re-layouts  12.4 us (10%)
  other arithmetic  7.44 us (6%)
    ppermute x25, waiting for transfers between devices, send(): return lax.ppermute(array, AXES, pairs)  52.2 us
    ppermute x25, starting transfers between devices, send(): return lax.ppermute(array, AXES, pairs)  25.4 us
    pallas_call x1, Pallas kernels, on_device(): pl.pallas_call(functools.partial(attend_kernel, m, count), out_shape=jax....  11.6 us
    pallas_call x1, Pallas kernels, on_device(): pl.pallas_call(functools.partial(project_kernel, chips_z, count), out_sha...  9.23 us
    transpose x1, other arithmetic, on_device(): normed = normed.reshape(count, chunks, rows).transpose(1, 0, 2)  4.69 us
    convert_element_type x1, local copies, waits for them, and re-layouts, on_device(): inputs = hidden[0].astype(jnp.float32)  3.25 us
    unnamed x19, local copies, waits for them, and re-layouts  3.01 us
  transfers between devices with their start and end apart: 25, of which 10 were waited for; matrix products, arithmetic and copies ran while one was open for 7% of the time, Pallas kernels for 8%

profile of v1, /device:TPU:24, one launch (start us, length us, event | category | flops | bytes accessed | tf_op | source)
XLA Modules:
  0.0 118.6 jit_solution(481529891899660541)
XLA Ops:
  0.0 3.0 %copy.9 = bf16[1,256,5120]{1,2,0:T(8,128)(2,1)S(1)} copy(bf16[1,256,5120]{2,1,0:T(8,128)(2,1)} %param.8) | data formatting | bytes 5242880 | tf_op args[0]
  3.0 0.7 multiply_reduce_fusion
  3.7 3.2 %copy.10 = f32[256,8,640]{2,0,1:T(8,128)} copy(bf16[256,8,640]{0,2,1:T(8,128)(2,1)S(1)} %bitcast.21) | data formatting | bytes 7864320 | tf_op jit(solution)/shard_map/convert_element_type | solution.py:147
  7.0 4.7 %fusion.own = bf16[8,256,640]{2,1,0:T(8,128)(2,1)} fusion(f32[256,8,640]{2,0,1:T(8,128)} %copy.10, f32[8,640]{1,0:T(8,128)S(1)} %mul.50, f32[256]{0:T(256)S(1)} %add_rsqrt_fusion), kind=kLoop, calls=%fused_computation.2 | loop fusion | flops 3932160 | bytes 7885824 | tf_op jit(solution)/shard_map/transpose | solution.py:151
  11.9 0.3 pad_maximum_fusion
  12.2 0.4 reshape.70
  12.6 0.9 fusion.2
  13.7 0.6 collective-permute-start.3
  14.3 2.8 %collective-permute-done.3 = bf16[320,512]{1,0:T(8,128)(2,1)S(1)} collective-permute-done((bf16[320,512]{1,0:T(8,128)(2,1)S(1)}, bf16[320,512]{1,0:T(8,128)(2,1)S(1)}, u32[]{:S(2)}, u32[]{:S(2)}) %collective-permute-start.3) | collective-permute-done | bytes 327712 | tf_op jit(solution)/shard_map/ppermute | solution.py:120
  17.1 0.2 maximum_select_fusion
  17.4 1.7 %collective-permute-start.4 = (bf16[640,256]{1,0:T(8,128)(2,1)S(1)}, bf16[640,256]{1,0:T(8,128)(2,1)S(1)}, u32[]{:S(2)}, u32[]{:S(2)}) collective-permute-start(bf16[640,256]{1,0:T(8,128)(2,1)S(1)} %get-tuple-element.12.rest_0_), channel_id=1, source_target_pairs={{0,4},{1,5},{2,6},{3,7},{4,0},{5,1},{6,2},{7,3},{8,12},{9,13},{10,... | collective-permute-start | bytes 983048 | tf_op jit(solution)/shard_map/ppermute | solution.py:120
  19.2 1.7 %collective-permute-start.12 = (bf16[640,256]{1,0:T(8,128)(2,1)S(1)}, bf16[640,256]{1,0:T(8,128)(2,1)S(1)}, u32[]{:S(2)}, u32[]{:S(2)}) collective-permute-start(bf16[640,256]{1,0:T(8,128)(2,1)S(1)} %get-tuple-element.12.rest_0_), channel_id=1, source_target_pairs={{0,16},{1,17},{2,18},{3,19},{4,20},{5,21},{6,22},{7,23},{8,24},{9,... | collective-permute-start | bytes 983048 | tf_op jit(solution)/shard_map/ppermute | solution.py:120
  20.9 1.2 %collective-permute-start.17 = (bf16[640,256]{1,0:T(8,128)(2,1)S(1)}, bf16[640,256]{1,0:T(8,128)(2,1)}, u32[]{:S(2)}, u32[]{:S(2)}) collective-permute-start(bf16[640,256]{1,0:T(8,128)(2,1)S(1)} %get-tuple-element.12.rest_0_), channel_id=1, source_target_pairs={{0,24},{1,25},{2,26},{3,27},{4,28},{5,29},{6,30},{7,31},{8,0},{9,1... | collective-permute-start | bytes 983048 | tf_op jit(solution)/shard_map/ppermute | solution.py:120
  22.1 5.3 %collective-permute-done.7.rest_5_ = bf16[640,256]{1,0:T(8,128)(2,1)S(1)} collective-permute-done((bf16[640,256]{1,0:T(8,128)(2,1)S(1)}, bf16[640,256]{1,0:T(8,128)(2,1)S(1)}, u32[]{:S(2)}, u32[]{:S(2)}) %collective-permute-start.7) | collective-permute-done | bytes 327712 | tf_op jit(solution)/shard_map/ppermute | solution.py:120
  27.4 1.5 %collective-permute-start.8 = (bf16[640,256]{1,0:T(8,128)(2,1)S(1)}, bf16[640,256]{1,0:T(8,128)(2,1)S(1)}, u32[]{:S(2)}, u32[]{:S(2)}) collective-permute-start(bf16[640,256]{1,0:T(8,128)(2,1)S(1)} %collective-permute-done.7.rest_5_), channel_id=1, source_target_pairs={{0,1},{1,0},{2,3},{3,2},{4,5},{5,4},{6,7},{7,6},{8,9},{9,8},{10,11... | collective-permute-start | bytes 983048 | tf_op jit(solution)/shard_map/ppermute | solution.py:120
  28.9 1.5 %collective-permute-start.9 = (bf16[640,256]{1,0:T(8,128)(2,1)S(1)}, bf16[640,256]{1,0:T(8,128)(2,1)S(1)}, u32[]{:S(2)}, u32[]{:S(2)}) collective-permute-start(bf16[640,256]{1,0:T(8,128)(2,1)S(1)} %collective-permute-done.7.rest_5_), channel_id=1, source_target_pairs={{0,4},{1,5},{2,6},{3,7},{4,0},{5,1},{6,2},{7,3},{8,12},{9,13},{10,... | collective-permute-start | bytes 983048 | tf_op jit(solution)/shard_map/ppermute | solution.py:120
  30.5 17.7 %collective-permute-done.12.rest_10_ = bf16[640,256]{1,0:T(8,128)(2,1)S(1)} collective-permute-done((bf16[640,256]{1,0:T(8,128)(2,1)S(1)}, bf16[640,256]{1,0:T(8,128)(2,1)S(1)}, u32[]{:S(2)}, u32[]{:S(2)}) %collective-permute-start.12) | collective-permute-done | bytes 327712 | tf_op jit(solution)/shard_map/ppermute | solution.py:120
  48.1 1.5 %collective-permute-start.13 = (bf16[640,256]{1,0:T(8,128)(2,1)S(1)}, bf16[640,256]{1,0:T(8,128)(2,1)S(1)}, u32[]{:S(2)}, u32[]{:S(2)}) collective-permute-start(bf16[640,256]{1,0:T(8,128)(2,1)S(1)} %collective-permute-done.12.rest_10_), channel_id=1, source_target_pairs={{0,1},{1,0},{2,3},{3,2},{4,5},{5,4},{6,7},{7,6},{8,9},{9,8},{10,11... | collective-permute-start | bytes 983048 | tf_op jit(solution)/shard_map/ppermute | solution.py:120
  49.6 1.5 %collective-permute-start.14 = (bf16[640,256]{1,0:T(8,128)(2,1)S(1)}, bf16[640,256]{1,0:T(8,128)(2,1)S(1)}, u32[]{:S(2)}, u32[]{:S(2)}) collective-permute-start(bf16[640,256]{1,0:T(8,128)(2,1)S(1)} %collective-permute-done.12.rest_10_), channel_id=1, source_target_pairs={{0,4},{1,5},{2,6},{3,7},{4,0},{5,1},{6,2},{7,3},{8,12},{9,13},{10,... | collective-permute-start | bytes 983048 | tf_op jit(solution)/shard_map/ppermute | solution.py:120
  51.1 0.5 collective-permute-start.18
  51.7 0.5 collective-permute-start.19
  52.2 0.7 fusion.3
  52.9 0.7 slice.66
  53.6 0.7 slice.67
  54.3 4.5 %collective-permute-done.13.rest_11_ = bf16[640,256]{1,0:T(8,128)(2,1)S(1)} collective-permute-done((bf16[640,256]{1,0:T(8,128)(2,1)S(1)}, bf16[640,256]{1,0:T(8,128)(2,1)S(1)}, u32[]{:S(2)}, u32[]{:S(2)}) %collective-permute-start.13) | collective-permute-done | bytes 327712 | tf_op jit(solution)/shard_map/ppermute | solution.py:120
  58.8 1.5 %collective-permute-start.5 = (bf16[320,256]{1,0:T(8,128)(2,1)}, bf16[320,256]{1,0:T(8,128)(2,1)S(1)}, u32[]{:S(2)}, u32[]{:S(2)}) collective-permute-start(bf16[320,256]{1,0:T(8,128)(2,1)} %get-tuple-element.16), channel_id=1, source_target_pairs={{0,1},{1,0},{2,3},{3,2},{4,5},{5,4},{6,7},{7,6},{8,9},{9,8},{10,11... | collective-permute-start | bytes 491528 | tf_op jit(solution)/shard_map/ppermute | solution.py:120
  60.3 0.5 collective-permute-start.6
  60.8 5.0 %collective-permute-done.18.rest_16_ = bf16[640,256]{1,0:T(8,128)(2,1)S(1)} collective-permute-done((bf16[640,256]{1,0:T(8,128)(2,1)}, bf16[640,256]{1,0:T(8,128)(2,1)S(1)}, u32[]{:S(2)}, u32[]{:S(2)}) %collective-permute-start.18) | collective-permute-done | bytes 327712 | tf_op jit(solution)/shard_map/ppermute | solution.py:120
  65.8 1.5 %collective-permute-start.10 = (bf16[320,256]{1,0:T(8,128)(2,1)}, bf16[320,256]{1,0:T(8,128)(2,1)}, u32[]{:S(2)}, u32[]{:S(2)}) collective-permute-start(bf16[320,256]{1,0:T(8,128)(2,1)} %slice.66), channel_id=1, source_target_pairs={{0,1},{1,0},{2,3},{3,2},{4,5},{5,4},{6,7},{7,6},{8,9},{9,8},{10,11... | collective-permute-start | bytes 491528 | tf_op jit(solution)/shard_map/ppermute | solution.py:120
  67.3 1.5 %collective-permute-start.11 = (bf16[320,256]{1,0:T(8,128)(2,1)}, bf16[320,256]{1,0:T(8,128)(2,1)}, u32[]{:S(2)}, u32[]{:S(2)}) collective-permute-start(bf16[320,256]{1,0:T(8,128)(2,1)} %slice.67), channel_id=1, source_target_pairs={{0,4},{1,5},{2,6},{3,7},{4,0},{5,1},{6,2},{7,3},{8,12},{9,13},{10,... | collective-permute-start | bytes 491528 | tf_op jit(solution)/shard_map/ppermute | solution.py:120
  68.9 0.8 copy.13.seg_q
  69.7 0.8 copy.14.pos_q
  70.5 0.9 slice.70
  71.5 0.6 collective-permute-start.15
  72.1 0.8 collective-permute-done.6.rest_4_
  72.9 1.5 %collective-permute-start.16 = (bf16[320,256]{1,0:T(8,128)(2,1)S(1)}, bf16[320,256]{1,0:T(8,128)(2,1)S(1)}, u32[]{:S(2)}, u32[]{:S(2)}) collective-permute-start(bf16[320,256]{1,0:T(8,128)(2,1)S(1)} %slice.69), channel_id=1, source_target_pairs={{0,4},{1,5},{2,6},{3,7},{4,0},{5,1},{6,2},{7,3},{8,12},{9,13},{10,... | collective-permute-start | bytes 491528 | tf_op jit(solution)/shard_map/ppermute | solution.py:120
  74.4 2.0 %collective-permute-done.10.rest_8_ = bf16[320,256]{1,0:T(8,128)(2,1)} collective-permute-done((bf16[320,256]{1,0:T(8,128)(2,1)}, bf16[320,256]{1,0:T(8,128)(2,1)}, u32[]{:S(2)}, u32[]{:S(2)}) %collective-permute-start.10) | collective-permute-done | bytes 163872 | tf_op jit(solution)/shard_map/ppermute | solution.py:120
  76.4 1.5 %collective-permute-start.20 = (bf16[320,256]{1,0:T(8,128)(2,1)S(1)}, bf16[320,256]{1,0:T(8,128)(2,1)S(1)}, u32[]{:S(2)}, u32[]{:S(2)}) collective-permute-start(bf16[320,256]{1,0:T(8,128)(2,1)S(1)} %slice.70), channel_id=1, source_target_pairs={{0,1},{1,0},{2,3},{3,2},{4,5},{5,4},{6,7},{7,6},{8,9},{9,8},{10,11... | collective-permute-start | bytes 491528 | tf_op jit(solution)/shard_map/ppermute | solution.py:120
  77.9 1.5 %collective-permute-start.21 = (bf16[320,256]{1,0:T(8,128)(2,1)S(1)}, bf16[320,256]{1,0:T(8,128)(2,1)S(1)}, u32[]{:S(2)}, u32[]{:S(2)}) collective-permute-start(bf16[320,256]{1,0:T(8,128)(2,1)S(1)} %slice.71), channel_id=1, source_target_pairs={{0,4},{1,5},{2,6},{3,7},{4,0},{5,1},{6,2},{7,3},{8,12},{9,13},{10,... | collective-permute-start | bytes 491528 | tf_op jit(solution)/shard_map/ppermute | solution.py:120
  79.5 1.0 fusion.1
  80.7 0.7 collective-permute-start
  81.3 0.4 collective-permute-done.20.rest_18_
  81.8 1.5 %collective-permute-done.21.rest_19_ = bf16[320,256]{1,0:T(8,128)(2,1)S(1)} collective-permute-done((bf16[320,256]{1,0:T(8,128)(2,1)S(1)}, bf16[320,256]{1,0:T(8,128)(2,1)S(1)}, u32[]{:S(2)}, u32[]{:S(2)}) %collective-permute-start.21) | collective-permute-done | bytes 163872 | tf_op jit(solution)/shard_map/ppermute | solution.py:120
  83.3 9.2 %project.1 = (bf16[256,512]{1,0:T(8,128)(2,1)S(1)}, bf16[256,512]{1,0:T(8,128)(2,1)S(1)}) custom-call(s32[3]{0:T(128)S(1)} %pad_add_fusion.3.place, bf16[8,256,640]{2,1,0:T(8,128)(2,1)} %fusion.own, bf16[8,256,640]{2,1,0:T(8,128)(2,1)} %collective-permute-done.1.other, f32[512,128]{1,0:T(8,128)S(1)} %get-tuple-element.22.cosine, ...), custom_call_target="tpu_custom_call" | custom-call | flops 2684354560 | bytes 10485760 | tf_op jit(solution)/shard_map/project/pallas_call | solution.py:181
  92.6 0.7 collective-permute-start.24
  93.3 1.5 %collective-permute-start.22 = (bf16[256,512]{1,0:T(8,128)(2,1)S(1)}, bf16[256,512]{1,0:T(8,128)(2,1)S(1)}, u32[]{:S(2)}, u32[]{:S(2)}) collective-permute-start(bf16[256,512]{1,0:T(8,128)(2,1)S(1)} %get-tuple-element.7.rest_0_), channel_id=1, source_target_pairs={{0,1},{1,0},{2,3},{3,2},{4,5},{5,4},{6,7},{7,6},{8,9},{9,8},{10,11... | collective-permute-start | bytes 786440 | tf_op jit(solution)/shard_map/ppermute | solution.py:120
  94.8 12.1 %collective-permute-done.22.rest_1_ = bf16[256,512]{1,0:T(8,128)(2,1)S(1)} collective-permute-done((bf16[256,512]{1,0:T(8,128)(2,1)S(1)}, bf16[256,512]{1,0:T(8,128)(2,1)S(1)}, u32[]{:S(2)}, u32[]{:S(2)}) %collective-permute-start.22) | collective-permute-done | bytes 262176 | tf_op jit(solution)/shard_map/ppermute | solution.py:120
  106.9 11.6 %attend.1 = bf16[256,4096]{1,0:T(8,128)(2,1)} custom-call(s32[1]{0:T(128)} %bitcast.place, bf16[256,4096]{1,0:T(8,128)(2,1)S(1)} %bitcast.20, s32[256,1]{1,0:T(8,128)S(1)} %copy-done, s32[256,1]{1,0:T(8,128)S(1)} %copy-done.1, s32[1,512]{1,0:T(1,128)S(1)} %pad_add_fusion.1.seg_k, s32[1,512]{1,0:T(1,128)S(1)} %pad_add_fusion.2.pos_k, ...), custom_call_target="tpu_custom_call" | custom-call | flops 2147483648 | bytes 4194304 | tf_op jit(solution)/shard_map/attend/pallas_call | solution.py:209
  (54 shorter events, 0.9 us)
Async XLA Ops:
  3.7 3.3 %copy-start.6 = (f32[5120]{0:T(1024)S(1)}, f32[5120]{0:T(1024)}, u32[]{:S(2)}) copy-start(f32[5120]{0:T(1024)} %param.10) | copy-start | bytes 61444
  7.0 4.7 %copy-start.4 = (bf16[320,512]{1,0:T(8,128)(2,1)S(1)}, bf16[320,512]{1,0:T(8,128)(2,1)}, u32[]{:S(2)}) copy-start(bf16[320,512]{1,0:T(8,128)(2,1)} %param.13) | copy-start | bytes 983044
  7.0 4.8 %copy-start.5 = (bf16[320,512]{1,0:T(8,128)(2,1)S(1)}, bf16[320,512]{1,0:T(8,128)(2,1)}, u32[]{:S(2)}) copy-start(bf16[320,512]{1,0:T(8,128)(2,1)} %param.12) | copy-start | bytes 983044
  11.7 71.6 %collective-permute-start.1 = (bf16[8,256,640]{2,1,0:T(8,128)(2,1)}, bf16[8,256,640]{2,1,0:T(8,128)(2,1)}, u32[]{:S(2)}, u32[]{:S(2)}) collective-permute-start(bf16[8,256,640]{2,1,0:T(8,128)(2,1)} %fusion.own), channel_id=1, source_target_pairs={{0,2},{1,3},{2,0},{3,1},{4,6},{5,7},{6,4},{7,5},{8,10},{9,11},{10,... | collective-permute-start | bytes 7864328 | tf_op jit(solution)/shard_map/ppermute | solution.py:120
  13.6 5.6 %copy-start.7 = (s32[1,256]{1,0:T(1,128)S(1)}, s32[1,256]{1,0:T(1,128)}, u32[]{:S(2)}) copy-start(s32[1,256]{1,0:T(1,128)} %param.15) | copy-start | bytes 3076
  13.6 16.9 %copy-start.8 = (s32[1,256]{1,0:T(1,128)S(1)}, s32[1,256]{1,0:T(1,128)}, u32[]{:S(2)}) copy-start(s32[1,256]{1,0:T(1,128)} %param.14) | copy-start | bytes 3076
  13.7 3.4 %collective-permute-start.3 = (bf16[320,512]{1,0:T(8,128)(2,1)S(1)}, bf16[320,512]{1,0:T(8,128)(2,1)S(1)}, u32[]{:S(2)}, u32[]{:S(2)}) collective-permute-start(bf16[320,512]{1,0:T(8,128)(2,1)S(1)} %get-tuple-element.10), channel_id=1, source_target_pairs={{0,2},{1,3},{2,0},{3,1},{4,6},{5,7},{6,4},{7,5},{8,10},{9,11},{10,... | collective-permute-start | bytes 983048 | tf_op jit(solution)/shard_map/ppermute | solution.py:120
  17.4 65.9 %copy-start.2 = (f32[128]{0:T(128)S(1)}, f32[128]{0:T(128)}, u32[]{:S(2)}) copy-start(f32[128]{0:T(128)} %param.11) | copy-start | bytes 1540
  17.4 10.1 %collective-permute-start.7 = (bf16[640,256]{1,0:T(8,128)(2,1)S(1)}, bf16[640,256]{1,0:T(8,128)(2,1)S(1)}, u32[]{:S(2)}, u32[]{:S(2)}) collective-permute-start(bf16[640,256]{1,0:T(8,128)(2,1)S(1)} %get-tuple-element.12.rest_0_), channel_id=1, source_target_pairs={{0,8},{1,9},{2,10},{3,11},{4,12},{5,13},{6,14},{7,15},{8,16},{9,17... | collective-permute-start | bytes 983048 | tf_op jit(solution)/shard_map/ppermute | solution.py:120
  17.4 11.5 %collective-permute-start.4 = (bf16[640,256]{1,0:T(8,128)(2,1)S(1)}, bf16[640,256]{1,0:T(8,128)(2,1)S(1)}, u32[]{:S(2)}, u32[]{:S(2)}) collective-permute-start(bf16[640,256]{1,0:T(8,128)(2,1)S(1)} %get-tuple-element.12.rest_0_), channel_id=1, source_target_pairs={{0,4},{1,5},{2,6},{3,7},{4,0},{5,1},{6,2},{7,3},{8,12},{9,13},{10,... | collective-permute-start | bytes 983048 | tf_op jit(solution)/shard_map/ppermute | solution.py:120
  19.2 1.7 %collective-permute-start.2 = (s32[1,256]{1,0:T(1,128)S(1)}, s32[1,256]{1,0:T(1,128)S(1)}, u32[]{:S(2)}, u32[]{:S(2)}) collective-permute-start(s32[1,256]{1,0:T(1,128)S(1)} %copy-done.7), channel_id=1, source_target_pairs={{0,2},{1,3},{2,0},{3,1},{4,6},{5,7},{6,4},{7,5},{8,10},{9,11},{10,... | collective-permute-start | bytes 3080 | tf_op jit(solution)/shard_map/ppermute | solution.py:120
  19.2 29.0 %collective-permute-start.12 = (bf16[640,256]{1,0:T(8,128)(2,1)S(1)}, bf16[640,256]{1,0:T(8,128)(2,1)S(1)}, u32[]{:S(2)}, u32[]{:S(2)}) collective-permute-start(bf16[640,256]{1,0:T(8,128)(2,1)S(1)} %get-tuple-element.12.rest_0_), channel_id=1, source_target_pairs={{0,16},{1,17},{2,18},{3,19},{4,20},{5,21},{6,22},{7,23},{8,24},{9,... | collective-permute-start | bytes 983048 | tf_op jit(solution)/shard_map/ppermute | solution.py:120
  20.9 28.8 %collective-permute-start.17 = (bf16[640,256]{1,0:T(8,128)(2,1)S(1)}, bf16[640,256]{1,0:T(8,128)(2,1)}, u32[]{:S(2)}, u32[]{:S(2)}) collective-permute-start(bf16[640,256]{1,0:T(8,128)(2,1)S(1)} %get-tuple-element.12.rest_0_), channel_id=1, source_target_pairs={{0,24},{1,25},{2,26},{3,27},{4,28},{5,29},{6,30},{7,31},{8,0},{9,1... | collective-permute-start | bytes 983048 | tf_op jit(solution)/shard_map/ppermute | solution.py:120
  27.4 23.7 %collective-permute-start.8 = (bf16[640,256]{1,0:T(8,128)(2,1)S(1)}, bf16[640,256]{1,0:T(8,128)(2,1)S(1)}, u32[]{:S(2)}, u32[]{:S(2)}) collective-permute-start(bf16[640,256]{1,0:T(8,128)(2,1)S(1)} %collective-permute-done.7.rest_5_), channel_id=1, source_target_pairs={{0,1},{1,0},{2,3},{3,2},{4,5},{5,4},{6,7},{7,6},{8,9},{9,8},{10,11... | collective-permute-start | bytes 983048 | tf_op jit(solution)/shard_map/ppermute | solution.py:120
  28.9 22.7 %collective-permute-start.9 = (bf16[640,256]{1,0:T(8,128)(2,1)S(1)}, bf16[640,256]{1,0:T(8,128)(2,1)S(1)}, u32[]{:S(2)}, u32[]{:S(2)}) collective-permute-start(bf16[640,256]{1,0:T(8,128)(2,1)S(1)} %collective-permute-done.7.rest_5_), channel_id=1, source_target_pairs={{0,4},{1,5},{2,6},{3,7},{4,0},{5,1},{6,2},{7,3},{8,12},{9,13},{10,... | collective-permute-start | bytes 983048 | tf_op jit(solution)/shard_map/ppermute | solution.py:120
  48.1 10.6 %collective-permute-start.13 = (bf16[640,256]{1,0:T(8,128)(2,1)S(1)}, bf16[640,256]{1,0:T(8,128)(2,1)S(1)}, u32[]{:S(2)}, u32[]{:S(2)}) collective-permute-start(bf16[640,256]{1,0:T(8,128)(2,1)S(1)} %collective-permute-done.12.rest_10_), channel_id=1, source_target_pairs={{0,1},{1,0},{2,3},{3,2},{4,5},{5,4},{6,7},{7,6},{8,9},{9,8},{10,11... | collective-permute-start | bytes 983048 | tf_op jit(solution)/shard_map/ppermute | solution.py:120
  49.6 10.6 %collective-permute-start.14 = (bf16[640,256]{1,0:T(8,128)(2,1)S(1)}, bf16[640,256]{1,0:T(8,128)(2,1)S(1)}, u32[]{:S(2)}, u32[]{:S(2)}) collective-permute-start(bf16[640,256]{1,0:T(8,128)(2,1)S(1)} %collective-permute-done.12.rest_10_), channel_id=1, source_target_pairs={{0,4},{1,5},{2,6},{3,7},{4,0},{5,1},{6,2},{7,3},{8,12},{9,13},{10,... | collective-permute-start | bytes 983048 | tf_op jit(solution)/shard_map/ppermute | solution.py:120
  51.1 14.7 %collective-permute-start.18 = (bf16[640,256]{1,0:T(8,128)(2,1)}, bf16[640,256]{1,0:T(8,128)(2,1)S(1)}, u32[]{:S(2)}, u32[]{:S(2)}) collective-permute-start(bf16[640,256]{1,0:T(8,128)(2,1)} %collective-permute-done.17.rest_15_), channel_id=1, source_target_pairs={{0,1},{1,0},{2,3},{3,2},{4,5},{5,4},{6,7},{7,6},{8,9},{9,8},{10,11... | collective-permute-start | bytes 983048 | tf_op jit(solution)/shard_map/ppermute | solution.py:120
  51.7 15.6 %collective-permute-start.19 = (bf16[640,256]{1,0:T(8,128)(2,1)}, bf16[640,256]{1,0:T(8,128)(2,1)}, u32[]{:S(2)}, u32[]{:S(2)}) collective-permute-start(bf16[640,256]{1,0:T(8,128)(2,1)} %collective-permute-done.17.rest_15_), channel_id=1, source_target_pairs={{0,4},{1,5},{2,6},{3,7},{4,0},{5,1},{6,2},{7,3},{8,12},{9,13},{10,... | collective-permute-start | bytes 983048 | tf_op jit(solution)/shard_map/ppermute | solution.py:120
  58.8 12.7 %collective-permute-start.5 = (bf16[320,256]{1,0:T(8,128)(2,1)}, bf16[320,256]{1,0:T(8,128)(2,1)S(1)}, u32[]{:S(2)}, u32[]{:S(2)}) collective-permute-start(bf16[320,256]{1,0:T(8,128)(2,1)} %get-tuple-element.16), channel_id=1, source_target_pairs={{0,1},{1,0},{2,3},{3,2},{4,5},{5,4},{6,7},{7,6},{8,9},{9,8},{10,11... | collective-permute-start | bytes 491528 | tf_op jit(solution)/shard_map/ppermute | solution.py:120
  60.3 12.7 %collective-permute-start.6 = (bf16[320,256]{1,0:T(8,128)(2,1)}, bf16[320,256]{1,0:T(8,128)(2,1)}, u32[]{:S(2)}, u32[]{:S(2)}) collective-permute-start(bf16[320,256]{1,0:T(8,128)(2,1)} %get-tuple-element.15), channel_id=1, source_target_pairs={{0,1},{1,0},{2,3},{3,2},{4,5},{5,4},{6,7},{7,6},{8,9},{9,8},{10,11... | collective-permute-start | bytes 491528 | tf_op jit(solution)/shard_map/ppermute | solution.py:120
  65.8 10.6 %collective-permute-start.10 = (bf16[320,256]{1,0:T(8,128)(2,1)}, bf16[320,256]{1,0:T(8,128)(2,1)}, u32[]{:S(2)}, u32[]{:S(2)}) collective-permute-start(bf16[320,256]{1,0:T(8,128)(2,1)} %slice.66), channel_id=1, source_target_pairs={{0,1},{1,0},{2,3},{3,2},{4,5},{5,4},{6,7},{7,6},{8,9},{9,8},{10,11... | collective-permute-start | bytes 491528 | tf_op jit(solution)/shard_map/ppermute | solution.py:120
  67.3 10.6 %collective-permute-start.11 = (bf16[320,256]{1,0:T(8,128)(2,1)}, bf16[320,256]{1,0:T(8,128)(2,1)}, u32[]{:S(2)}, u32[]{:S(2)}) collective-permute-start(bf16[320,256]{1,0:T(8,128)(2,1)} %slice.67), channel_id=1, source_target_pairs={{0,4},{1,5},{2,6},{3,7},{4,0},{5,1},{6,2},{7,3},{8,12},{9,13},{10,... | collective-permute-start | bytes 491528 | tf_op jit(solution)/shard_map/ppermute | solution.py:120
  71.5 9.2 %collective-permute-start.15 = (bf16[320,256]{1,0:T(8,128)(2,1)S(1)}, bf16[320,256]{1,0:T(8,128)(2,1)S(1)}, u32[]{:S(2)}, u32[]{:S(2)}) collective-permute-start(bf16[320,256]{1,0:T(8,128)(2,1)S(1)} %slice.68), channel_id=1, source_target_pairs={{0,1},{1,0},{2,3},{3,2},{4,5},{5,4},{6,7},{7,6},{8,9},{9,8},{10,11... | collective-permute-start | bytes 491528 | tf_op jit(solution)/shard_map/ppermute | solution.py:120
  72.9 8.4 %collective-permute-start.16 = (bf16[320,256]{1,0:T(8,128)(2,1)S(1)}, bf16[320,256]{1,0:T(8,128)(2,1)S(1)}, u32[]{:S(2)}, u32[]{:S(2)}) collective-permute-start(bf16[320,256]{1,0:T(8,128)(2,1)S(1)} %slice.69), channel_id=1, source_target_pairs={{0,4},{1,5},{2,6},{3,7},{4,0},{5,1},{6,2},{7,3},{8,12},{9,13},{10,... | collective-permute-start | bytes 491528 | tf_op jit(solution)/shard_map/ppermute | solution.py:120
  76.4 5.3 %collective-permute-start.20 = (bf16[320,256]{1,0:T(8,128)(2,1)S(1)}, bf16[320,256]{1,0:T(8,128)(2,1)S(1)}, u32[]{:S(2)}, u32[]{:S(2)}) collective-permute-start(bf16[320,256]{1,0:T(8,128)(2,1)S(1)} %slice.70), channel_id=1, source_target_pairs={{0,1},{1,0},{2,3},{3,2},{4,5},{5,4},{6,7},{7,6},{8,9},{9,8},{10,11... | collective-permute-start | bytes 491528 | tf_op jit(solution)/shard_map/ppermute | solution.py:120
  77.9 5.3 %collective-permute-start.21 = (bf16[320,256]{1,0:T(8,128)(2,1)S(1)}, bf16[320,256]{1,0:T(8,128)(2,1)S(1)}, u32[]{:S(2)}, u32[]{:S(2)}) collective-permute-start(bf16[320,256]{1,0:T(8,128)(2,1)S(1)} %slice.71), channel_id=1, source_target_pairs={{0,4},{1,5},{2,6},{3,7},{4,0},{5,1},{6,2},{7,3},{8,12},{9,13},{10,... | collective-permute-start | bytes 491528 | tf_op jit(solution)/shard_map/ppermute | solution.py:120
  80.7 14.1 %collective-permute-start = (s32[2,256]{1,0:T(2,128)S(1)}, s32[2,256]{1,0:T(2,128)S(1)}, u32[]{:S(2)}, u32[]{:S(2)}) collective-permute-start(s32[2,256]{1,0:T(2,128)S(1)} %pad_add_fusion), channel_id=1, source_target_pairs={{0,1},{1,0},{2,3},{3,2},{4,5},{5,4},{6,7},{7,6},{8,9},{9,8},{10,11... | collective-permute-start | bytes 6152 | tf_op jit(solution)/shard_map/ppermute | solution.py:120
  83.3 23.6 %copy-start = (s32[256,1]{1,0:T(8,128)S(1)}, s32[256,1]{1,0:T(8,128)}, u32[]{:S(2)}) copy-start(s32[256,1]{1,0:T(8,128)} %copy.13.seg_q) | copy-start | bytes 3076
  83.3 23.6 %copy-start.1 = (s32[256,1]{1,0:T(8,128)S(1)}, s32[256,1]{1,0:T(8,128)}, u32[]{:S(2)}) copy-start(s32[256,1]{1,0:T(8,128)} %copy.14.pos_q) | copy-start | bytes 3076
  83.3 23.6 %copy-start.3 = (bf16[1,256,4096]{2,1,0:T(8,128)(2,1)S(1)}, bf16[1,256,4096]{2,1,0:T(8,128)(2,1)}, u32[]{:S(2)}) copy-start(bf16[1,256,4096]{2,1,0:T(8,128)(2,1)} %param.9) | copy-start | bytes 6291460
  92.5 14.4 %collective-permute-start.23 = (bf16[256,512]{1,0:T(8,128)(2,1)S(1)}, bf16[256,512]{1,0:T(8,128)(2,1)S(1)}, u32[]{:S(2)}, u32[]{:S(2)}) collective-permute-start(bf16[256,512]{1,0:T(8,128)(2,1)S(1)} %get-tuple-element.8), channel_id=1, source_target_pairs={{0,2},{1,3},{2,0},{3,1},{4,6},{5,7},{6,4},{7,5},{8,10},{9,11},{10,... | collective-permute-start | bytes 786440 | tf_op jit(solution)/shard_map/ppermute | solution.py:120
  92.6 14.3 %collective-permute-start.24 = (bf16[256,512]{1,0:T(8,128)(2,1)S(1)}, bf16[256,512]{1,0:T(8,128)(2,1)S(1)}, u32[]{:S(2)}, u32[]{:S(2)}) collective-permute-start(bf16[256,512]{1,0:T(8,128)(2,1)S(1)} %get-tuple-element.8), channel_id=1, source_target_pairs={{0,3},{1,2},{2,1},{3,0},{4,7},{5,6},{6,5},{7,4},{8,11},{9,10},{10,... | collective-permute-start | bytes 786440 | tf_op jit(solution)/shard_map/ppermute | solution.py:120
  93.3 13.6 %collective-permute-start.22 = (bf16[256,512]{1,0:T(8,128)(2,1)S(1)}, bf16[256,512]{1,0:T(8,128)(2,1)S(1)}, u32[]{:S(2)}, u32[]{:S(2)}) collective-permute-start(bf16[256,512]{1,0:T(8,128)(2,1)S(1)} %get-tuple-element.7.rest_0_), channel_id=1, source_target_pairs={{0,1},{1,0},{2,3},{3,2},{4,5},{5,4},{6,7},{7,6},{8,9},{9,8},{10,11... | collective-permute-start | bytes 786440 | tf_op jit(solution)/shard_map/ppermute | solution.py:120

commit v2 on v0

v2 whole, which is shorter than its diff:
```python
import functools
import math

import jax
import jax.numpy as jnp
import numpy as np
from jax import lax
from jax.experimental import pallas as pl
from jax.experimental.pallas import tpu as pltpu
from jax.sharding import Mesh
from jax.sharding import PartitionSpec as P

KVH = 4
HD = 128
G = 8
EPS = 1e-06
THETA = 1000000.0
MASKED = -1e30
VMEM_LIMIT = 48 * 2**20


def project_kernel(count, own, other, weight, cosine, sine, gain, kv_own, kv_other, acc):
    step = pl.program_id(0)
    for part, lhs in enumerate((own, other)):
        at = pl.ds(part * count, count)
        for half in range(2):
            term = jnp.dot(
                lhs[step], weight[0, half], preferred_element_type=jnp.float32
            )

            @pl.when(step == 0)
            def _():
                acc[half, at, :] = term

            @pl.when(step > 0)
            def _():
                acc[half, at, :] += term

    @pl.when(step == pl.num_programs(0) - 1)
    def _():
        for part, out in enumerate((kv_own, kv_other)):
            at = pl.ds(part * count, count)
            raw = acc[0, at, :]
            normk = raw * lax.rsqrt(jnp.mean(raw * raw, axis=-1, keepdims=True) + EPS) * gain[...]
            turned = normk * cosine[at, :] + pltpu.roll(normk, HD // 2, 1) * sine[at, :]
            out[:, :HD] = turned.astype(jnp.bfloat16)
            out[:, HD:] = acc[1, at, :].astype(jnp.bfloat16)


def attend_kernel(pieces, count, place, queries, seg_q, pos_q, seg_k, pos_k, *rest):
    sources, (out, bias, keys, values) = rest[: 2 * pieces], rest[-4:]
    step = pl.program_id(0)

    @pl.when(step == 0)
    def _():
        allowed = (seg_k[...] == seg_q[...]) & (pos_k[...] <= pos_q[...])
        bias[...] = jnp.where(allowed, 0.0, MASKED)

    for at in range(2):

        @pl.when(step == at)
        def _():
            for i in range(pieces):
                source = sources[at * pieces + i]
                keys[i * count : (i + 1) * count, :] = source[:, :HD]
                values[i * count : (i + 1) * count, :] = source[:, HD:]

    factor = math.log2(math.e) / math.sqrt(HD)
    for g in range(G):
        part = slice(g * HD, (g + 1) * HD)
        scores = lax.dot_general(
            queries[:, part], keys[...], (((1,), (1,)), ((), ())),
            preferred_element_type=jnp.float32,
        ) + bias[...]
        top = jnp.max(scores, axis=-1, keepdims=True)
        weights = jnp.exp2((scores - top) * factor)
        total = jnp.sum(weights, axis=-1, keepdims=True)
        summed = jnp.dot(
            weights.astype(jnp.bfloat16), values[...], preferred_element_type=jnp.float32
        )
        out[:, part] = (summed * (1.0 / total)).astype(jnp.bfloat16)


def swap(array, axis):
    return lax.ppermute(array, axis, [(0, 1), (1, 0)])


def on_device(
    sizes, hidden, queries, norm_gain, key_gain, k_weight, v_weight, segment, position
):
    chips_z, groups = sizes[0], sizes[3]
    count, width = hidden.shape[1:]
    own_rows = k_weight.shape[0]
    rows = 2 * own_rows
    chunks = 2 * chips_z
    m = 2 * groups
    core, x = lax.axis_index("core"), lax.axis_index("x")
    bf16 = jnp.bfloat16

    def along_ctx(array, d, cross=False):
        pairs = []
        for c in range(2):
            for i in range(m):
                pairs.append((c * m + i, (c ^ int(cross)) * m + (i + d) % m))
        return lax.ppermute(array, ("core", "ctx", "x"), pairs)

    def columns(which):
        at = which * 2 * HD
        return jnp.stack(
            [lax.dynamic_slice_in_dim(w, at, 2 * HD, 1) for w in (k_weight, v_weight)]
        )

    taken = swap(columns(1 - core), "core")
    kept = columns(core)
    chip = lax.dynamic_update_slice(
        jnp.zeros((2, rows, 2 * HD), bf16), kept, (0, core * own_rows, 0)
    )
    chip = lax.dynamic_update_slice(chip, taken, (0, (1 - core) * own_rows, 0))
    mine = lax.dynamic_index_in_dim(chip, x, 0, keepdims=False)
    gathered = [
        lax.all_gather(mine[:, s * HD : (s + 1) * HD], ("z", "y", "x")).reshape(
            chunks, 2, rows, HD
        )
        for s in range(2)
    ]

    hidden, taken = lax.optimization_barrier((hidden, taken))
    inputs = hidden[0].astype(jnp.float32)
    normed = (
        inputs * lax.rsqrt(jnp.mean(inputs * inputs, axis=-1, keepdims=True) + EPS) * norm_gain
    ).astype(bf16)
    normed = normed.reshape(count, chunks, rows).transpose(1, 0, 2)
    normed_other = swap(normed, "core")

    ints = jnp.concatenate([segment, position])
    ints_all = [ints] + [along_ctx(ints, d) for d in range(1, m)]
    where = jnp.concatenate([position[0], swap(position, "core")[0]]).astype(jnp.float32)
    half = HD // 2
    freq = np.exp(np.arange(half, dtype=np.float32) * np.float32(-2.0 * math.log(THETA) / HD))
    angle = where[:, None] * freq[None, :]
    cosine, sine = jnp.cos(angle), jnp.sin(angle)
    cosine = jnp.concatenate([cosine, cosine], axis=1)
    sine = jnp.concatenate([-sine, sine], axis=1)
    seg_k = jnp.concatenate([piece[:1] for piece in ints_all], axis=1)
    pos_k = jnp.concatenate([piece[1:] for piece in ints_all], axis=1)

    whole = pl.BlockSpec(memory_space=pltpu.VMEM)
    place = core.astype(jnp.int32)[None]
    params = pltpu.CompilerParams(vmem_limit_bytes=VMEM_LIMIT)
    result = None
    for s in range(2):
        kv_own, kv_other = pl.pallas_call(
            functools.partial(project_kernel, count),
            out_shape=[jax.ShapeDtypeStruct((count, 2 * HD), bf16)] * 2,
            grid=(chunks,),
            in_specs=[
                whole,
                whole,
                pl.BlockSpec((1, 2, rows, HD), lambda i: (i, 0, 0, 0)),
                whole,
                whole,
                whole,
            ],
            out_specs=[whole] * 2,
            scratch_shapes=[pltpu.VMEM((2, 2 * count, HD), jnp.float32)],
            compiler_params=params,
            cost_estimate=pl.CostEstimate(
                flops=2 * 2 * count * width * 2 * HD,
                bytes_accessed=2 * width * (2 * count + 2 * HD),
                transcendentals=0,
            ),
            name="project",
        )(normed, normed_other, gathered[s], cosine, sine, key_gain[None])

        sources = [kv_own] + [along_ctx(kv_own, d) for d in range(1, m)]
        sources += [along_ctx(kv_other, d, True) for d in range(m)]

        def block(step, place, s=s):
            return (0, lax.rem(place[0] + step, 2) * 2 + s)

        earlier = [] if result is None else [result]
        result = pl.pallas_call(
            functools.partial(attend_kernel, m, count),
            out_shape=jax.ShapeDtypeStruct((count, KVH * G * HD), bf16),
            grid_spec=pltpu.PrefetchScalarGridSpec(
                num_scalar_prefetch=1,
                grid=(2,),
                in_specs=[pl.BlockSpec((count, G * HD), block)]
                + [whole] * (4 + 2 * m)
                + [pl.BlockSpec(memory_space=pl.ANY)] * len(earlier),
                out_specs=pl.BlockSpec((count, G * HD), block),
                scratch_shapes=[
                    pltpu.VMEM((count, m * count), jnp.float32),
                    pltpu.VMEM((m * count, HD), bf16),
                    pltpu.VMEM((m * count, HD), bf16),
                ],
            ),
            input_output_aliases={6 + 2 * m: 0} if earlier else {},
            compiler_params=params,
            cost_estimate=pl.CostEstimate(
                flops=2 * count * m * count * KVH * G * HD,
                bytes_accessed=2 * count * KVH * G * HD,
                transcendentals=count * m * count * KVH * G // 2,
            ),
            name="attend",
        )(
            place,
            queries[0],
            segment.reshape(count, 1),
            position.reshape(count, 1),
            seg_k,
            pos_k,
            *sources,
            *earlier,
        )
    return result[None]


def solution(mesh):
    n, m = mesh.shape["fsdp"], mesh.shape["ctx"]
    sizes = (n // 4, 2, 2, m // 2, 2)
    fine = Mesh(mesh.devices.reshape(sizes), ("z", "y", "core", "ctx", "x"))
    fsdp, ctx = ("z", "y", "core"), ("ctx", "x")
    placed = (
        P(fsdp, ctx, None),
        P(fsdp, ctx, None),
        P(),
        P(),
        P(fsdp, None),
        P(fsdp, None),
        P(fsdp, ctx),
        P(fsdp, ctx),
    )
    return jax.shard_map(
        functools.partial(on_device, sizes),
        mesh=fine,
        in_specs=placed,
        out_specs=P(fsdp, ctx, None),
        check_vma=False,
    )
```

time: 163 us -> 177 us (1.086)
  Pallas kernels: 0 us -> 35.4 us
  blocking collectives: 28.3 us -> 0 us
  waiting for transfers between devices: 82.2 us -> 105 us
  matrix products: 19.2 us -> 0 us
  starting transfers between devices: 0.04 us -> 8.5 us
  local copies, waits for them, and re-layouts: 12.8 us -> 9.2 us
    pallas_call x0 -> x4, Pallas kernels: none -> 35.4 us  [the longest x2 21.9 us: on_device(): pl.pallas_call(functools.partial(project_kernel, count), out_shape=[jax.S...]
    all_gather x4 -> x0, blocking collectives: 28.3 us -> none  [the longest x1 9.33 us: on_device(): value_piece = lax.all_gather(values[None], 'ctx', axis=1, tiled=True)]
    all_gather x2, waiting for transfers between devices: 80.8 us -> 102 us  [on_device(): lax.all_gather(mine[:, s * HD:(s + 1) * HD], ('z', 'y', 'x'))]
    dot_general x4 -> x0, matrix products: 19.2 us -> none  [the longest x1 5.62 us: on_device(): jnp.dot(normed, lax.all_gather(v_weight, 'fsdp', axis=0, tiled=True), pre...]
    ppermute x0 -> x10, starting transfers between devices: none -> 8.45 us  [the longest x7 7.36 us: along_ctx(): return lax.ppermute(array, ('core', 'ctx', 'x'), pairs)]
    dot_general x1 -> x0, local copies, waits for them, and re-layouts: 7.9 us -> none  [on_device(): jnp.dot(normed, lax.all_gather(k_weight, 'fsdp', axis=0, tiled=True), pre...]
    reduce_sum x1 -> x0, other arithmetic: 4.2 us -> none  [on_device(): total = jnp.sum(weights, axis=-1)]
    transpose x0 -> x1, other arithmetic: none -> 3.14 us  [on_device(): normed = normed.reshape(count, chunks, rows).transpose(1, 0, 2)]
  transfers between devices with their start and end apart: 2 -> 12, of which waited for: 2 -> 4; matrix products, arithmetic and copies ran while one was open for 11% -> 7% of each run, Pallas kernels for 0% -> 17%
where the time goes in v2:
time: 177 us
  waiting for transfers between devices  105 us (59%)
  Pallas kernels  35.4 us (20%)
  between operations  13.6 us (8%)
  local copies, waits for them, and re-layouts  9.2 us (5%)
  starting transfers between devices  8.5 us (5%)
  other arithmetic  5.14 us (3%)
    all_gather x2, waiting for transfers between devices, on_device(): lax.all_gather(mine[:, s * HD:(s + 1) * HD], ('z', 'y', 'x'))  102 us
    pallas_call x2, Pallas kernels, on_device(): pl.pallas_call(functools.partial(project_kernel, count), out_shape=[jax.S...  21.9 us
    pallas_call x2, Pallas kernels, on_device(): pl.pallas_call(functools.partial(attend_kernel, m, count), out_shape=jax....  13.5 us
    ppermute x7, starting transfers between devices, along_ctx(): return lax.ppermute(array, ('core', 'ctx', 'x'), pairs)  7.36 us
  transfers between devices with their start and end apart: 12, of which 4 were waited for; matrix products, arithmetic and copies ran while one was open for 7% of the time, Pallas kernels for 17%

profile of v2, /device:TPU:0, one launch (start us, length us, event | category | flops | bytes accessed | tf_op | source)
XLA Modules:
  0.0 176.5 jit_solution(8009283129846537723)
XLA Ops:
  6.5 0.0 all-gather.7.cloned.1.call-start
  6.5 1.2 dynamic-slice_bitcast_fusion.1
  7.8 0.5 collective-permute-start.1
  8.4 1.2 collective-permute-done.1
  9.6 0.7 fusion.2
  10.4 0.0 all-gather.7.cloned.1.call-update
  10.4 0.0 all-gather.5.cloned.1.call-start
  10.4 0.7 all-gather.5.cloned.1.call-update
  11.2 0.0 copy-done.2
  11.2 3.0 %copy.11 = bf16[1,256,5120]{1,2,0:T(8,128)(2,1)S(1)} copy(bf16[1,256,5120]{2,1,0:T(8,128)(2,1)} %param.9) | data formatting | bytes 5242880 | tf_op jit(solution)/shard_map/optimization_barrier | solution.py:127
  14.2 3.3 %copy.12 = f32[256,8,640]{2,0,1:T(8,128)} copy(bf16[256,8,640]{0,2,1:T(8,128)(2,1)S(1)} %bitcast.28) | data formatting | bytes 7864320 | tf_op jit(solution)/shard_map/convert_element_type | solution.py:128
  17.4 0.7 multiply_reduce_fusion
  18.1 0.0 copy-start.4
  18.1 0.0 copy-start.7
  18.2 0.0 copy-start.1
  18.2 3.1 %fusion.own = bf16[8,256,640]{2,1,0:T(8,128)(2,1)S(1)} fusion(f32[256,8,640]{2,0,1:T(8,128)} %copy.12, f32[8,640]{1,0:T(8,128)S(1)} %mul.57, f32[256]{0:T(256)S(1)} %add_rsqrt_fusion), kind=kLoop, calls=%fused_computation.2 | loop fusion | flops 3932160 | bytes 7885824 | tf_op jit(solution)/shard_map/transpose | solution.py:132
  21.3 0.4 collective-permute-start.2
  21.8 0.1 collective-permute-start.3
  21.9 3.0 %collective-permute-start = (s32[2,256]{1,0:T(2,128)S(1)}, s32[2,256]{1,0:T(2,128)S(1)}, u32[]{:S(2)}, u32[]{:S(2)}) collective-permute-start(s32[2,256]{1,0:T(2,128)S(1)} %pad_add_fusion), channel_id=1, source_target_pairs={{0,1},{1,0},{2,3},{3,2},{4,5},{5,4},{6,7},{7,6},{8,9},{9,8},{10,11... | collective-permute-start | bytes 6152 | tf_op jit(solution)/shard_map/ppermute | solution.py:105
  24.9 0.1 copy.15.seg_q
  25.1 0.1 copy.16.pos_q
  25.2 1.1 collective-permute-done.3
  26.3 1.0 fusion.1
  27.3 0.2 pad_maximum_fusion.1
  27.5 0.0 collective-permute-done
  27.5 0.6 fusion.3
  28.1 0.0 collective-permute-done.2.other
  28.1 49.0 %all-gather.7.cloned.1.call-done = bf16[10240,128]{1,0:T(8,128)(2,1)} async-done(((bf16[640,128]{1,0:T(8,128)(2,1)}), bf16[10240,128]{1,0:T(8,128)(2,1)}) %all-gather.7.cloned.1.call-update) | async-done | bytes 2621456 | tf_op jit(solution)/shard_map/all_gather | solution.py:121
  77.1 11.2 %project.3 = (bf16[256,256]{1,0:T(8,128)(2,1)S(1)}, bf16[256,256]{1,0:T(8,128)(2,1)}) custom-call(bf16[8,256,640]{2,1,0:T(8,128)(2,1)S(1)} %fusion.own, bf16[8,256,640]{2,1,0:T(8,128)(2,1)} %collective-permute-done.2.other, bf16[8,2,640,128]{3,2,1,0:T(8,128)(2,1)} %bitcast.30, f32[512,128]{1,0:T(8,128)S(1)} %get-tuple-element.28.cosine, ...), custom_call_target="tpu_custom_call" | custom-call | flops 1342177280 | bytes 7864320 | tf_op jit(solution)/shard_map/project/pallas_call | solution.py:152
  88.3 1.4 collective-permute-start.7
  89.7 0.0 copy-done.6
  89.8 0.0 collective-permute-start.8
  89.8 0.7 collective-permute-start.9
  90.5 52.7 %all-gather.5.cloned.1.call-done = bf16[10240,128]{1,0:T(8,128)(2,1)} async-done(((bf16[640,128]{1,0:T(8,128)(2,1)}), bf16[10240,128]{1,0:T(8,128)(2,1)}) %all-gather.5.cloned.1.call-update) | async-done | bytes 2621456 | tf_op jit(solution)/shard_map/all_gather | solution.py:121
  143.2 10.7 %project.2 = (bf16[256,256]{1,0:T(8,128)(2,1)S(1)}, bf16[256,256]{1,0:T(8,128)(2,1)S(1)}) custom-call(bf16[8,256,640]{2,1,0:T(8,128)(2,1)S(1)} %fusion.own, bf16[8,256,640]{2,1,0:T(8,128)(2,1)} %collective-permute-done.2.other, bf16[8,2,640,128]{3,2,1,0:T(8,128)(2,1)} %bitcast.29, f32[512,128]{1,0:T(8,128)S(1)} %get-tuple-element.28.cosine, ...), custom_call_target="tpu_custom_call" | custom-call | flops 1342177280 | bytes 7864320 | tf_op jit(solution)/shard_map/project/pallas_call | solution.py:152
  153.9 0.1 collective-permute-start.5
  154.0 1.6 collective-permute-start.6
  155.5 0.0 collective-permute-done.7.rest_1_
  155.5 0.6 collective-permute-start.4
  156.1 0.0 copy-done.5
  156.1 0.0 collective-permute-done.8.rest_2_
  156.1 0.0 collective-permute-done.9.rest_3_
  156.1 0.0 copy-done
  156.1 7.3 %attend.2.rest_4_ = bf16[256,4096]{1,0:T(8,128)(2,1)} custom-call(s32[1]{0:T(128)} %bitcast.place, bf16[256,4096]{1,0:T(8,128)(2,1)S(1)} %bitcast.24, s32[256,1]{1,0:T(8,128)S(1)} %copy.15.seg_q, s32[256,1]{1,0:T(8,128)S(1)} %copy.16.pos_q, s32[1,512]{1,0:T(1,128)S(1)} %pad_add_fusion.1.seg_k, s32[1,512]{1,0:T(1,128)S(1)} %pad_add_fusion.2.pos_k, ...), custom_call_target="tpu_custom_call" | custom-call | flops 1073741824 | bytes 2097152 | tf_op jit(solution)/shard_map/attend/pallas_call | solution.py:182
  163.4 0.0 collective-permute-done.4.rest_1_
  163.4 0.0 collective-permute-done.5.rest_2_
  163.4 0.0 collective-permute-done.6.rest_3_
  163.4 6.3 %attend.3 = bf16[256,4096]{1,0:T(8,128)(2,1)} custom-call(s32[1]{0:T(128)} %bitcast.place, bf16[256,4096]{1,0:T(8,128)(2,1)S(1)} %bitcast.25, s32[256,1]{1,0:T(8,128)S(1)} %copy.15.seg_q, s32[256,1]{1,0:T(8,128)S(1)} %copy.16.pos_q, s32[1,512]{1,0:T(1,128)S(1)} %pad_add_fusion.1.seg_k, ...), custom_call_target="tpu_custom_call", output_to_operand_aliasing={{}: (10, {})} | custom-call | flops 1073741824 | bytes 2097152 | tf_op jit(solution)/shard_map/attend/pallas_call | solution.py:182
  (20 shorter events, 0.2 us)
Async XLA Ops:
  6.5 70.6 %all-gather.7.cloned.1.call-start = ((), (), s32[]{:S(2)}) async-start(), calls=%async_computation.1 | async-start | bytes 2785280 | tf_op jit(solution)/shard_map/all_gather | solution.py:121
  6.5 4.6 %copy-start.2 = (f32[5120]{0:T(1024)S(1)}, f32[5120]{0:T(1024)}, u32[]{:S(2)}) copy-start(f32[5120]{0:T(1024)} %param.11) | copy-start | bytes 61444
  7.8 1.8 %collective-permute-start.1 = (bf16[2,320,256]{2,1,0:T(8,128)(2,1)S(1)}, bf16[2,320,256]{2,1,0:T(8,128)(2,1)S(1)}, u32[]{:S(2)}, u32[]{:S(2)}) collective-permute-start(bf16[2,320,256]{2,1,0:T(8,128)(2,1)S(1)} %pad_maximum_fusion), channel_id=1, source_target_pairs={{0,2},{2,0},{1,3},{3,1},{4,6},{6,4},{5,7},{7,5},{8,10},{10,8},{9,1... | collective-permute-start | bytes 983048 | tf_op jit(solution)/shard_map/ppermute | solution.py:85
  10.4 132.8 %all-gather.5.cloned.1.call-start = ((), (), s32[]{:S(2)}) async-start(), calls=%async_computation | async-start | bytes 2785280 | tf_op jit(solution)/shard_map/all_gather | solution.py:121
  18.1 3.6 %copy-start.3 = (s32[1,256]{1,0:T(1,128)S(1)}, s32[1,256]{1,0:T(1,128)}, u32[]{:S(2)}) copy-start(s32[1,256]{1,0:T(1,128)} %param.16) | copy-start | bytes 3076
  18.1 3.8 %copy-start.4 = (s32[1,256]{1,0:T(1,128)S(1)}, s32[1,256]{1,0:T(1,128)}, u32[]{:S(2)}) copy-start(s32[1,256]{1,0:T(1,128)} %param.15) | copy-start | bytes 3076
  18.1 8.1 %copy-start.7 = (f32[64]{0:T(128)S(1)}, f32[64]{0:T(128)}, u32[]{:S(2)}) copy-start(f32[64]{0:T(128)} %constant.42) | copy-start | bytes 772
  18.2 58.9 %copy-start.1 = (f32[128]{0:T(128)S(1)}, f32[128]{0:T(128)}, u32[]{:S(2)}) copy-start(f32[128]{0:T(128)} %param.12) | copy-start | bytes 1540
  21.3 6.8 %collective-permute-start.2 = (bf16[8,256,640]{2,1,0:T(8,128)(2,1)S(1)}, bf16[8,256,640]{2,1,0:T(8,128)(2,1)}, u32[]{:S(2)}, u32[]{:S(2)}) collective-permute-start(bf16[8,256,640]{2,1,0:T(8,128)(2,1)S(1)} %fusion.own), channel_id=1, source_target_pairs={{0,2},{2,0},{1,3},{3,1},{4,6},{6,4},{5,7},{7,5},{8,10},{10,8},{9,1... | collective-permute-start | bytes 7864328 | tf_op jit(solution)/shard_map/ppermute | solution.py:85
  21.8 4.5 %collective-permute-start.3 = (s32[1,256]{1,0:T(1,128)S(1)}, s32[1,256]{1,0:T(1,128)S(1)}, u32[]{:S(2)}, u32[]{:S(2)}) collective-permute-start(s32[1,256]{1,0:T(1,128)S(1)} %copy-done.3), channel_id=1, source_target_pairs={{0,2},{2,0},{1,3},{3,1},{4,6},{6,4},{5,7},{7,5},{8,10},{10,8},{9,1... | collective-permute-start | bytes 3080 | tf_op jit(solution)/shard_map/ppermute | solution.py:85
  21.9 5.6 %collective-permute-start = (s32[2,256]{1,0:T(2,128)S(1)}, s32[2,256]{1,0:T(2,128)S(1)}, u32[]{:S(2)}, u32[]{:S(2)}) collective-permute-start(s32[2,256]{1,0:T(2,128)S(1)} %pad_add_fusion), channel_id=1, source_target_pairs={{0,1},{1,0},{2,3},{3,2},{4,5},{5,4},{6,7},{7,6},{8,9},{9,8},{10,11... | collective-permute-start | bytes 6152 | tf_op jit(solution)/shard_map/ppermute | solution.py:105
  77.1 12.6 %copy-start.6 = (s32[1,256]{1,0:T(1,128)S(1)}, s32[1,256]{1,0:T(1,128)}, u32[]{:S(2)}) copy-start(s32[1,256]{1,0:T(1,128)} %get-tuple-element.25) | copy-start | bytes 3076
  88.3 67.2 %collective-permute-start.7 = (bf16[256,256]{1,0:T(8,128)(2,1)S(1)}, bf16[256,256]{1,0:T(8,128)(2,1)}, u32[]{:S(2)}, u32[]{:S(2)}) collective-permute-start(bf16[256,256]{1,0:T(8,128)(2,1)S(1)} %get-tuple-element.13.rest_0_), channel_id=1, source_target_pairs={{0,1},{1,0},{2,3},{3,2},{4,5},{5,4},{6,7},{7,6},{8,9},{9,8},{10,11... | collective-permute-start | bytes 393224 | tf_op jit(solution)/shard_map/ppermute | solution.py:105
  89.8 66.4 %collective-permute-start.8 = (bf16[256,256]{1,0:T(8,128)(2,1)}, bf16[256,256]{1,0:T(8,128)(2,1)}, u32[]{:S(2)}, u32[]{:S(2)}) collective-permute-start(bf16[256,256]{1,0:T(8,128)(2,1)} %get-tuple-element.14), channel_id=1, source_target_pairs={{0,2},{1,3},{2,0},{3,1},{4,6},{5,7},{6,4},{7,5},{8,10},{9,11},{10,... | collective-permute-start | bytes 393224 | tf_op jit(solution)/shard_map/ppermute | solution.py:105
  89.8 66.4 %collective-permute-start.9 = (bf16[256,256]{1,0:T(8,128)(2,1)}, bf16[256,256]{1,0:T(8,128)(2,1)}, u32[]{:S(2)}, u32[]{:S(2)}) collective-permute-start(bf16[256,256]{1,0:T(8,128)(2,1)} %get-tuple-element.14), channel_id=1, source_target_pairs={{0,3},{1,2},{2,1},{3,0},{4,7},{5,6},{6,5},{7,4},{8,11},{9,10},{10,... | collective-permute-start | bytes 393224 | tf_op jit(solution)/shard_map/ppermute | solution.py:105
  143.2 12.9 %copy-start.5 = (s32[1,256]{1,0:T(1,128)S(1)}, s32[1,256]{1,0:T(1,128)}, u32[]{:S(2)}) copy-start(s32[1,256]{1,0:T(1,128)} %get-tuple-element.24) | copy-start | bytes 3076
  143.2 12.9 %copy-start = (bf16[1,256,4096]{2,1,0:T(8,128)(2,1)S(1)}, bf16[1,256,4096]{2,1,0:T(8,128)(2,1)}, u32[]{:S(2)}) copy-start(bf16[1,256,4096]{2,1,0:T(8,128)(2,1)} %param.10) | copy-start | bytes 6291460
  153.9 9.5 %collective-permute-start.5 = (bf16[256,256]{1,0:T(8,128)(2,1)S(1)}, bf16[256,256]{1,0:T(8,128)(2,1)S(1)}, u32[]{:S(2)}, u32[]{:S(2)}) collective-permute-start(bf16[256,256]{1,0:T(8,128)(2,1)S(1)} %get-tuple-element.12), channel_id=1, source_target_pairs={{0,2},{1,3},{2,0},{3,1},{4,6},{5,7},{6,4},{7,5},{8,10},{9,11},{10,... | collective-permute-start | bytes 393224 | tf_op jit(solution)/shard_map/ppermute | solution.py:105
  154.0 9.5 %collective-permute-start.6 = (bf16[256,256]{1,0:T(8,128)(2,1)S(1)}, bf16[256,256]{1,0:T(8,128)(2,1)S(1)}, u32[]{:S(2)}, u32[]{:S(2)}) collective-permute-start(bf16[256,256]{1,0:T(8,128)(2,1)S(1)} %get-tuple-element.12), channel_id=1, source_target_pairs={{0,3},{1,2},{2,1},{3,0},{4,7},{5,6},{6,5},{7,4},{8,11},{9,10},{10,... | collective-permute-start | bytes 393224 | tf_op jit(solution)/shard_map/ppermute | solution.py:105
  155.5 7.9 %collective-permute-start.4 = (bf16[256,256]{1,0:T(8,128)(2,1)S(1)}, bf16[256,256]{1,0:T(8,128)(2,1)S(1)}, u32[]{:S(2)}, u32[]{:S(2)}) collective-permute-start(bf16[256,256]{1,0:T(8,128)(2,1)S(1)} %get-tuple-element.11.rest_0_), channel_id=1, source_target_pairs={{0,1},{1,0},{2,3},{3,2},{4,5},{5,4},{6,7},{7,6},{8,9},{9,8},{10,11... | collective-permute-start | bytes 393224 | tf_op jit(solution)/shard_map/ppermute | solution.py:105
Sparse Core Ops, SparseCore 0:
  10.5 66.5 all-gather.6
  79.8 63.3 all-gather.4
